TPU v7x, 512 devices: a whole 4x8x8 slice. The times are simulated.
512 devices in a mesh: space: 64 (over x, y, z_hi), tm: 8 (over z_lo, core).
Axes of the slice: x: 4, y: 8, z: 8 (z_hi: 2, z_lo: 4; z = z_hi * 4 + z_lo), core: 2. Of those that a mesh axis runs over, the one named last changes fastest.
Arguments:
- links: float32 [4, 2, 3, 3, 128, 16, 128], P(None, None, None, None, 'space', 'tm'), as said below
- kernel: float32 [3, 3, 3, 3, 4, 8], replicated, may hold values from -0.25 to 0.25
- active: int32 [128, 16, 128], P('space', 'tm'), may hold values 0 or 1
- direction: int32 [128, 16, 128], P('space', 'tm'), may hold values from 0 to 3
- out_grad: float32 [4, 2, 3, 3, 128, 16, 128], P(None, None, None, None, 'space', 'tm'), may hold values from -6 to 6
Outputs:
- link_grad: float32 [4, 2, 3, 3, 128, 16, 128], P(None, None, None, None, 'space', 'tm')
- kernel_grad: float32 [3, 3, 3, 3, 4, 8], replicated
Inputs may be any that keep to these rules, and one draw needn't show every extreme that they name: `links`: every link is special unitary: its rows are orthonormal and its third row is the complex conjugate of the cross product of its first two rows, up to float32 rounding.
All inputs are finite; a program needn't handle non-finite values. No bound on the sum of `active` on one device may be relied on, other than what follows from the above.
Results may differ from a plain program's by a relative error of at most 0.0003.
Values sent between devices are 32-bit elements; how exact they have to be, the bound alone decides.
A program may use at most 128 MiB of HBM per device.

v0:
```python
import functools
import math

import jax
import jax.numpy as jnp
from jax import lax
from jax.experimental import pallas as pl
from jax.experimental.pallas import tpu as pltpu
from jax.sharding import PartitionSpec as P

PAIR = (1, 0, 3, 2)
MESH = pl.DeviceIdType.MESH
F32 = jnp.float32
NEIGHBOURS = tuple((sx, st) for sx in (-1, 0, 1) for st in (-1, 0, 1) if (sx, st) != (0, 0))
FACES = ((-1, 0), (1, 0), (0, -1), (0, 1))
CORNERS = ((1, -1), (-1, 1))
GROWS = 24


def row_of(ext_x, ext_t):
    return 2 + 4 * ext_x + ext_t


def lane_iota(shape):
    return lax.broadcasted_iota(jnp.int32, shape, len(shape) - 1)


def half_mask(shape):
    return ((lax.broadcasted_iota(jnp.int32, shape, len(shape) - 2) >> 1) & 1) == 1


def roll_y(values, step):
    return pltpu.roll(values, (-16 * step) % 128, values.ndim - 1)


def roll_z(values, step):
    axis = values.ndim - 1
    z_coord = lane_iota(values.shape) & 15
    if step == 1:
        return jnp.where(z_coord == 15, pltpu.roll(values, 15, axis), pltpu.roll(values, 127, axis))
    return jnp.where(z_coord == 0, pltpu.roll(values, 113, axis), pltpu.roll(values, 1, axis))


def shift_yz(values, step_y, step_z):
    if step_y:
        values = roll_y(values, step_y)
    if step_z:
        values = roll_z(values, step_z)
    return values


def swap_halves(values):
    axis = values.ndim - 2
    return jnp.where(
        half_mask(values.shape), pltpu.roll(values, 2, axis), pltpu.roll(values, 6, axis)
    )


def split_roll(values, lead, step):
    along_y = roll_y(values, step)
    along_z = roll_z(values, step)
    first, second = (along_y, along_z) if lead == 2 else (along_z, along_y)
    return jnp.where(half_mask(values.shape), second, first)


def rolled(matrix, lead, step):
    return tuple(split_roll(part, lead, step) for part in matrix)


def mul(first, second, adj_first=False, adj_second=False):
    def column(part, k):
        return jnp.expand_dims(part[k] if adj_first else part[:, k], 1)

    def line(part, k):
        return jnp.expand_dims(part[:, k] if adj_second else part[k], 0)

    sums = [None] * 4
    for k in range(3):
        fr, fi = column(first[0], k), column(first[1], k)
        sr, si = line(second[0], k), line(second[1], k)
        terms = (fr * sr, fi * si, fr * si, fi * sr)
        sums = [t if s is None else s + t for s, t in zip(sums, terms)]
    rr, ii, ri, ir = sums
    real = rr + ii if adj_first != adj_second else rr - ii
    if adj_first and adj_second:
        imag = -(ri + ir)
    elif adj_first:
        imag = ri - ir
    elif adj_second:
        imag = ir - ri
    else:
        imag = ri + ir
    return (real, imag)


def add(first, second):
    return (first[0] + second[0], first[1] + second[1])


def scaled(matrix, factor):
    return (matrix[0] * factor, matrix[1] * factor)


def view(ref, course, dx, dt):
    start = row_of(1 + dx, 1 + dt)
    pair_start = row_of(1 + dt, 1 + dx) - 2
    parts = []
    for part in range(2):
        own = ref[course, part, :, :, pl.ds(start, 8), :]
        other = ref[PAIR[course], part, :, :, pl.ds(pair_start, 8), :]
        parts.append(jnp.where(half_mask(own.shape), other, own))
    return tuple(parts)


def view_at(ref, course, lead, step):
    if lead == 0:
        return view(ref, course, step, 0)
    if lead == 1:
        return view(ref, course, 0, step)
    return rolled(view(ref, course, 0, 0), lead, step)


ORDER = ((2, 3), (0, 1), (0, 2), (0, 3), (2, 0), (2, 1))


def legs_above(ref, course, across):
    return (
        view_at(ref, across, course, 1),
        view_at(ref, course, across, 1),
        view(ref, across, 0, 0),
    )


def legs_below(ref, course, across):
    if across >= 2:
        return (
            view(ref, course, 0, 0),
            view_at(ref, across, course, 1),
            view(ref, across, 0, 0),
        )
    back = (-1, 0) if across == 0 else (0, -1)
    base = view(ref, across, *back)
    if course >= 2:
        ahead = rolled(base, course, 1)
    else:
        step = (back[0] + (course == 0), back[1] + (course == 1))
        ahead = view(ref, across, *step)
    return (view(ref, course, *back), ahead, base)


def third_line(first, second):
    out = []
    for j in range(3):
        p, q = (j + 1) % 3, (j + 2) % 3
        (ar, ai), (br, bi) = first[p], second[q]
        (cr, ci), (dr, di) = first[q], second[p]
        real = (ar * br - ai * bi) - (cr * dr - ci * di)
        imag = (ar * bi + ai * br) - (cr * di + ci * dr)
        out.append((real, -imag))
    return out


def body(
    sizes, links, taps, active, direction, out_grad, link_grad, kernel_grad,
    ext, send_t0, send_t1, send_c, recv_x0, recv_x1, recv_t0, recv_t1, recv_c,
    mids, tap_rows, feats, feat_rows, trace_rows, small, k_rows, k_ext, g_ext, g_rows,
    code_ext, x_rows, x_mat, dressed, part, red_a, red_b, red_c, total,
    link_send, link_recv, feat_send, feat_recv, g_send, g_recv, k_send, k_recv,
    red_send, red_recv,
):
    n_space, n_tm, n_low, scale = sizes
    n_high = n_space // n_low
    my_x, my_t = lax.axis_index("space"), lax.axis_index("tm")
    low, high = lax.rem(my_x, n_low), lax.div(my_x, n_low)
    own_chunks = 8 // n_tm

    def device(sx, st):
        return (lax.rem(my_x + sx + n_space, n_space), lax.rem(my_t + st + n_tm, n_tm))

    def tm_peer(k):
        return (my_x, lax.rem(my_t + k, n_tm))

    def low_peer(k):
        return (high * n_low + lax.rem(low + k, n_low), my_t)

    def high_peer(k):
        return (lax.rem(high + k, n_high) * n_low + low, my_t)

    peers = [device(sx, st) for sx, st in NEIGHBOURS]
    peers += [tm_peer(k) for k in range(2, n_tm - 1)]
    peers += [low_peer(k) for k in range(1, n_low)]
    peers += [high_peer(k) for k in range(1, n_high)]
    barrier = pltpu.get_barrier_semaphore()
    for peer in peers:
        pl.semaphore_signal(barrier, inc=1, device_id=peer, device_id_type=MESH)

    for x in range(2):
        send_t0[:, :, :, :, x : x + 1, :] = links[:, :, 0:2, :, x, 1:2, :]
        send_t1[0:1, :, :, :, x : x + 1, :] = links[0:1, :, 0:2, :, x, 0:1, :]
        send_t1[1:3, :, :, :, x : x + 1, :] = links[2:4, :, 0:2, :, x, 0:1, :]
    send_c[0] = links[1, :, 0:2, :, 0, 1:2, :]
    send_c[1] = links[0, :, 0:2, :, 1, 0:1, :]

    pl.semaphore_wait(barrier, len(peers))

    def remote(source, target, send_sem, recv_sem, peer):
        return pltpu.make_async_remote_copy(
            src_ref=source, dst_ref=target, send_sem=send_sem, recv_sem=recv_sem,
            device_id=peer, device_id_type=MESH,
        )

    def start_all(copies):
        for copy in copies:
            copy.start()
        return copies

    def finish(copies):
        for copy in copies:
            copy.wait_recv()

    plan = (
        (links.at[:, :, 0:2, :, 1], recv_x0, (1, 0)),
        (links.at[1:4, :, 0:2, :, 0], recv_x1, (-1, 0)),
        (send_c.at[0], recv_c.at[0], (-1, 1)),
        (send_c.at[1], recv_c.at[1], (1, -1)),
        (send_t0, recv_t0, (0, 1)),
        (send_t1, recv_t1, (0, -1)),
    )
    link_copies = start_all(
        [
            remote(source, target, link_send.at[i], link_recv.at[i], device(*step))
            for i, (source, target, step) in enumerate(plan)
        ]
    )

    ext[:, :, :, :, pl.ds(row_of(1, 1), 2), :] = links[:, :, :, :, 0]
    ext[:, :, :, :, pl.ds(row_of(2, 1), 2), :] = links[:, :, :, :, 1]

    diagonal = lax.broadcasted_iota(jnp.int32, (8, 8), 0) == lax.broadcasted_iota(
        jnp.int32, (8, 8), 1
    )

    def spread_taps(j, carry):
        for dxdt in range(9):
            block = taps[dxdt * 9 + j]
            for o in range(4):
                line = jnp.broadcast_to(block[o : o + 1, :], (8, 8))
                column = jnp.sum(jnp.where(diagonal, line, 0.0), axis=1, keepdims=True)
                tap_rows[j, dxdt * 4 + o] = jnp.broadcast_to(column, (8, 128))
        return carry

    lax.fori_loop(0, 9, spread_taps, 0)

    hid = (lax.broadcasted_iota(jnp.int32, (8, 128), 0) >> 1) & 1
    course_of = jnp.concatenate([direction[0], direction[0], direction[1], direction[1]], axis=0)
    moving = jnp.concatenate([active[0], active[0], active[1], active[1]], axis=0)
    moves = moving.astype(F32)
    frozen_third = (1.0 - moves) * (1.0 / 3.0)
    chosen_of = {0: course_of == hid, 2: course_of == hid + 2}

    def stored(index):
        return (mids[index, 0], mids[index, 1])

    def store_mid(index, matrix):
        mids[index, 0] = matrix[0]
        mids[index, 1] = matrix[1]

    staples = {0: None, 2: None}

    def forward(number):
        course, across = ORDER[number]
        b, c, e = legs_above(ext, course, across)
        upper = mul(b, c, adj_second=True)
        store_mid(2 * number, upper)
        above = mul(upper, e, adj_second=True)
        a, b, e = legs_below(ext, course, across)
        lower = mul(a, b)
        store_mid(2 * number + 1, lower)
        below = mul(lower, e, adj_first=True)
        if across >= 2:
            below = rolled(below, across, -1)
        both = add(above, below)
        staples[course] = both if staples[course] is None else add(staples[course], both)

    forward(0)

    finish(link_copies)

    def fill(buffer, courses, put):
        lines = [
            [(buffer[:, 0, i, j], buffer[:, 1, i, j]) for j in range(3)] for i in range(2)
        ]
        lines.append(third_line(*lines))
        for i in range(3):
            for j in range(3):
                for k in range(2):
                    put(courses, k, i, j, lines[i][j][k])

    def put_x(ext_x):
        def put(courses, k, i, j, value):
            for n, course in enumerate(courses):
                ext[course, k, i, j, pl.ds(row_of(ext_x, 1), 2), :] = value[n]

        return put

    def put_t(ext_t):
        def put(courses, k, i, j, value):
            for n, course in enumerate(courses):
                for x in range(2):
                    ext[course, k, i, j, pl.ds(row_of(1 + x, ext_t), 1), :] = value[n, x : x + 1]

        return put

    def put_c(courses, k, i, j, value):
        ext[1, k, i, j, pl.ds(row_of(3, 0), 1), :] = value[0]
        ext[0, k, i, j, pl.ds(row_of(0, 3), 1), :] = value[1]

    fill(recv_x0, (0, 1, 2, 3), put_x(0))
    fill(recv_x1, (1, 2, 3), put_x(3))
    fill(recv_t0, (0, 1, 2, 3), put_t(0))
    fill(recv_t1, (0, 2, 3), put_t(3))
    fill(recv_c, (1, 0), put_c)

    for number in range(1, 6):
        forward(number)

    def trace(part):
        return part[0, 0] + part[1, 1] + part[2, 2]

    cores = {lead: view(ext, lead, 0, 0) for lead in (0, 2)}
    closed = {lead: mul(cores[lead], staples[lead]) for lead in (0, 2)}
    for lead in (0, 2):
        for k in range(2):
            value = trace(closed[lead][k]) * frozen_third
            trace_rows[pl.ds((2 * lead + k) * 8, 8), :] = value
            trace_rows[pl.ds((2 * lead + 2 + k) * 8, 8), :] = swap_halves(value)
    for x in range(2):
        for t in range(2):
            feats[1 + x, 1 + t] = trace_rows[pl.ds(4 * x + t, 8, 8), :]

    def edge(step):
        source = {1: pl.ds(2, 1), -1: pl.ds(1, 1), 0: pl.ds(1, 2)}[step]
        target = {1: pl.ds(0, 1), -1: pl.ds(3, 1), 0: pl.ds(1, 2)}[step]
        return source, target

    def edge_copies(ref, steps, send_sem, recv_sem):
        copies = []
        for i, (sx, st) in enumerate(steps):
            (from_x, to_x), (from_t, to_t) = edge(sx), edge(st)
            copies.append(
                remote(
                    ref.at[from_x, from_t], ref.at[to_x, to_t],
                    send_sem.at[i], recv_sem.at[i], device(sx, st),
                )
            )
        return start_all(copies)

    feat_copies = edge_copies(feats, NEIGHBOURS, feat_send, feat_recv)

    def roll_features(positions):
        for ext_x, ext_t in positions:
            value = feats[ext_x, ext_t]
            for dy in range(3):
                along_y = shift_yz(value, dy - 1, 0)
                for dz in range(3):
                    feat_rows[dy * 3 + dz, ext_x * 4 + ext_t] = shift_yz(along_y, 0, dz - 1)

    inner = [(x, t) for x in (1, 2) for t in (1, 2)]
    outer = [(x, t) for x in range(4) for t in range(4) if (x, t) not in inner]
    roll_features(inner)

    grads = {}
    for lead in (0, 2):
        grads[lead] = tuple(
            jnp.concatenate(
                [
                    out_grad[lead, k, :, :, 0],
                    out_grad[lead + 1, k, :, :, 0],
                    out_grad[lead, k, :, :, 1],
                    out_grad[lead + 1, k, :, :, 1],
                ],
                axis=2,
            )
            for k in range(2)
        )

    def choose(field):
        out = []
        for k in range(2):
            first, second = field[0][k], field[2][k]
            mask_first = jnp.broadcast_to(chosen_of[0].astype(F32), first.shape)
            mask_second = jnp.broadcast_to(chosen_of[2].astype(F32), first.shape)
            picked = first * mask_first + second * mask_second
            out.append(picked + swap_halves(picked))
        return tuple(out)

    def project(matrix):
        real, imag = matrix
        third = trace(imag) * (1.0 / 3.0)
        out = []
        for i, j in ((0, 1), (0, 2), (1, 2)):
            out.append((real[i, j] - real[j, i]) * 0.5)
            out.append((imag[i, j] + imag[j, i]) * 0.5)
        return out + [imag[0, 0] - third, imag[1, 1] - third]

    def expand(parts):
        r01, i01, r02, i02, r12, i12, d0, d1 = parts
        zero = jnp.zeros_like(d0)
        real = jnp.stack(
            [
                jnp.stack([zero, r01, r02]),
                jnp.stack([-r01, zero, r12]),
                jnp.stack([-r02, -r12, zero]),
            ]
        )
        imag = jnp.stack(
            [
                jnp.stack([d0, i01, i02]),
                jnp.stack([i01, d1, i12]),
                jnp.stack([i02, i12, -d0 - d1]),
            ]
        )
        return (real, imag)

    picked_link = choose(cores)
    generator = expand(project(choose(closed)))
    minus = scaled(generator, -1.0)
    powers = [mul(choose(grads), picked_link, adj_second=True)]
    for _ in range(4):
        powers.append(mul(minus, powers[-1]))
    series = [powers[0]]
    for k in range(3):
        series.append(add(powers[k + 1], mul(series[-1], minus)))

    def inner_product(first, second):
        total_sum = None
        for k in range(2):
            for i in range(3):
                for j in range(3):
                    term = first[k][i, j] * second[k][i, j]
                    total_sum = term if total_sum is None else total_sum + term
        return total_sum

    slopes = [inner_product(powers[k], generator) for k in range(4)]
    turns = [project(matrix) for matrix in series]

    small[0] = course_of.astype(F32)

    finish(feat_copies)
    roll_features(outer)

    def conv_step(j, acc):
        acc = list(acc)
        for dx in range(3):
            for dt in range(3):
                for o in range(4):
                    tap = tap_rows[j, (dx * 3 + dt) * 4 + o]
                    for n in range(4):
                        x, t = n // 2, n % 2
                        acc[o * 4 + n] = acc[o * 4 + n] + tap * feat_rows[j, (x + dx) * 4 + t + dt]
        return tuple(acc)

    acc = lax.fori_loop(0, 9, conv_step, tuple(jnp.zeros((8, 128), F32) for _ in range(16)))
    for n in range(4):
        s = 4 * (n // 2) + n % 2
        course_row = jnp.broadcast_to(small[0, pl.ds(s, 1), :], (8, 128))
        picked = jnp.where(course_row == 0.0, acc[n], 0.0)
        for o in range(1, 4):
            picked = picked + jnp.where(course_row == float(o), acc[o * 4 + n], 0.0)
        field_row = jnp.sum(picked, axis=0, keepdims=True)
        small[1, pl.ds(s, 1), :] = field_row
        small[1, pl.ds(s + 2, 1), :] = field_row
    bent = jnp.tanh(small[1])
    strength = bent * moves
    c1, c2, c3, c4 = slopes
    slope = c1 + strength * (c2 + strength * (c3 * 0.5 + strength * (c4 * (1.0 / 6.0))))
    field_grad = moves * (1.0 - bent * bent) * slope
    code = jnp.where(moving == 1, course_of, -1).astype(F32)
    g_ext[1, 1] = jnp.where(hid == 0, field_grad, code)
    t1, t2, t3, t4 = turns
    for k in range(8):
        poly = t1[k] + strength * (
            t2[k] * 0.5 + strength * (t3[k] * (1.0 / 6.0) + strength * (t4[k] * (1.0 / 24.0)))
        )
        k_rows[pl.ds(8 * k, 8), :] = -strength * poly
    for x in range(2):
        for t in range(2):
            k_ext[1 + x, 1 + t] = k_rows[pl.ds(4 * x + t, 8, 8), :]

    g_copies = start_all(
        [
            remote(
                g_ext.at[1, 1], g_ext.at[1 - sx, 1 - st],
                g_send.at[i], g_recv.at[i], device(sx, st),
            )
            for i, (sx, st) in enumerate(NEIGHBOURS)
        ]
    )
    k_copies = edge_copies(k_ext, FACES + CORNERS, k_send, k_recv)

    small[2] = field_grad
    sub = lax.broadcasted_iota(jnp.int32, (8, 128), 0).astype(F32)
    wide = []
    for n in range(4):
        s = 4 * (n // 2) + n % 2
        course_row = jnp.broadcast_to(small[0, pl.ds(s, 1), :], (8, 128))
        grad_row = jnp.broadcast_to(small[2, pl.ds(s, 1), :], (8, 128))
        wide.append(jnp.where(course_row == sub, grad_row, 0.0))
    wide = jnp.concatenate(wide, axis=1)

    def tap_grad(j):
        lines = []
        for dx in range(3):
            for dt in range(3):
                lines.append(
                    jnp.concatenate(
                        [
                            feat_rows[j, (n // 2 + dx) * 4 + n % 2 + dt]
                            for n in range(4)
                        ],
                        axis=1,
                    )
                )
        return lax.dot_general(
            wide, jnp.concatenate(lines, axis=0), (((1,), (1,)), ((), ())),
            precision=lax.Precision.HIGHEST, preferred_element_type=F32,
        )

    part[...] = jnp.zeros((8, 8, 128), F32)

    def tap_step(j, carry):
        part[j, :, 0:72] = tap_grad(j)
        return carry

    lax.fori_loop(0, 8, tap_step, 0)
    last = tap_grad(8)
    for o in range(4):
        part[o, 4:5, 0:72] = last[o : o + 1, :]

    red_a[my_t] = part[pl.ds(my_t * own_chunks, own_chunks)]
    base_a, base_b, base_c, base_d = 0, n_tm, n_tm + n_low, n_tm + n_low + n_high
    copies_a = []
    for k in range(1, n_tm):
        peer = tm_peer(k)
        copies_a.append(
            remote(
                part.at[pl.ds(peer[1] * own_chunks, own_chunks)], red_a.at[my_t],
                red_send.at[base_a + k], red_recv.at[base_a + k], peer,
            )
        )
    start_all(copies_a)

    decay = powers[4]
    blend = scaled(powers[4], 1.0 / 24.0)
    for k, factor in ((3, 1.0 / 6.0), (2, 0.5), (1, 1.0), (0, 1.0)):
        blend = add(scaled(blend, strength), scaled(powers[k], factor))
    straight = mul(blend, picked_link)

    finish(g_copies)

    whole = g_ext[...]
    axis = whole.ndim - 2
    mask = half_mask(whole.shape)
    values = jnp.where(mask, pltpu.roll(whole, 2, axis), whole)
    codes = jnp.where(mask, whole, pltpu.roll(whole, 6, axis))
    for pair in range(2):
        wanted = jnp.where(mask, 2.0 * pair + 1.0, 2.0 * pair)
        one = jnp.where(codes == wanted, values, 0.0)
        for dy in range(3):
            along_y = shift_yz(one, 1 - dy, 0)
            for dz in range(3):
                g_rows[dy * 3 + dz, pair] = shift_yz(along_y, 0, 1 - dz)

    spots = inner + [(0, 1), (0, 2), (3, 1), (3, 2), (1, 0), (2, 0), (1, 3), (2, 3), (3, 0), (0, 3)]

    def back_step(spot_list):
        def step(j, acc):
            acc = list(acc)
            for o in range(4):
                rows = {}
                for dx in range(3):
                    for dt in range(3):
                        tap = tap_rows[j, (dx * 3 + dt) * 4 + o]
                        for n, (ext_x, ext_t) in enumerate(spot_list):
                            px, pt = ext_x + 2 - dx, ext_t + 2 - dt
                            if (px, pt) not in rows:
                                s = 4 * (px % 2) + 2 * (o % 2) + pt % 2
                                rows[px, pt] = jnp.broadcast_to(
                                    g_rows[j, o // 2, px // 2, pt // 2, pl.ds(s, 1), :], (8, 128)
                                )
                            acc[n] = acc[n] + tap * rows[px, pt]
            return tuple(acc)

        return step

    spot_grad = lax.fori_loop(
        0, 9, back_step(spots), tuple(jnp.zeros((8, 128), F32) for _ in spots)
    )

    finish(k_copies)
    for n, (ext_x, ext_t) in enumerate(spots):
        block_x, block_t = (ext_x + 1) // 2, (ext_t + 1) // 2
        s = 4 * ((ext_x + 1) % 2) + 2 + (ext_t + 1) % 2
        code_row = g_ext[block_x, block_t, pl.ds(s, 1), :]
        code_ext[pl.ds(row_of(ext_x, ext_t), 1), :] = code_row
        merged = jnp.where(
            jnp.broadcast_to(code_row, (8, 128)) >= 0.0,
            k_ext[ext_x, ext_t],
            spot_grad[n] * (1.0 / 3.0),
        )
        x_rows[pl.ds(row_of(ext_x, ext_t), 8, GROWS), :] = merged

    for half in range(2):
        rows = pl.ds(2 + 8 * half, 8)
        code8 = code_ext[rows, :]
        parts = [x_rows[pl.ds(GROWS * k + 2 + 8 * half, 8), :] for k in range(8)]
        still = code8 < 0.0
        for course in range(4):
            turned = expand([jnp.where(code8 == float(course), p, 0.0) for p in parts])
            real, imag = turned
            one_real = jnp.where(still, parts[2 * course], 0.0)
            one_imag = jnp.where(still, parts[2 * course + 1], 0.0)
            zero = jnp.zeros_like(one_real)
            eye_real = jnp.stack(
                [jnp.stack([one_real if i == j else zero for j in range(3)]) for i in range(3)]
            )
            eye_imag = jnp.stack(
                [jnp.stack([one_imag if i == j else zero for j in range(3)]) for i in range(3)]
            )
            matrix = (real + eye_real, imag - eye_imag)
            product = mul(
                matrix, (ext[course, 0, :, :, rows, :], ext[course, 1, :, :, rows, :])
            )
            for k in range(2):
                x_mat[course, k, :, :, rows, :] = matrix[k]
                dressed[course, k, :, :, rows, :] = product[k]

    def reduce_step(copies, buffer):
        finish(copies)
        out = buffer[0]
        for k in range(1, buffer.shape[0]):
            out = out + buffer[k]
        return out

    red_b[low] = reduce_step(copies_a, red_a)
    copies_b = start_all(
        [
            remote(
                red_b.at[low], red_b.at[low],
                red_send.at[base_b + k], red_recv.at[base_b + k], low_peer(k),
            )
            for k in range(1, n_low)
        ]
    )

    link_sum = {0: None, 2: None}

    def backward(number):
        course, across = ORDER[number]
        b, c, e = legs_above(ext, course, across)
        db, dc, de = legs_above(dressed, course, across)
        upper = stored(2 * number)
        change = add(mul(db, c, adj_second=True), mul(b, dc, adj_second=True))
        above = add(mul(change, e, adj_second=True), mul(upper, de, adj_second=True))
        a, b, e = legs_below(ext, course, across)
        da, db, de = legs_below(dressed, course, across)
        lower = stored(2 * number + 1)
        change = add(mul(da, b), mul(a, db))
        below = add(mul(change, e, adj_first=True), mul(lower, de, adj_first=True))
        if across >= 2:
            below = rolled(below, across, -1)
        both = add(above, below)
        link_sum[course] = both if link_sum[course] is None else add(link_sum[course], both)

    for number in range(3):
        backward(number)

    red_c[high] = reduce_step(copies_b, red_b)
    copies_c = start_all(
        [
            remote(
                red_c.at[high], red_c.at[high],
                red_send.at[base_c + k], red_recv.at[base_c + k], high_peer(k),
            )
            for k in range(1, n_high)
        ]
    )

    for number in range(3, 6):
        backward(number)

    mine = pl.ds(my_t * own_chunks, own_chunks)
    total[mine] = reduce_step(copies_c, red_c) * scale
    copies_d = start_all(
        [
            remote(
                total.at[mine], total.at[mine],
                red_send.at[base_d + k], red_recv.at[base_d + k], tm_peer(k),
            )
            for k in range(1, n_tm)
        ]
    )

    for lead in (0, 2):
        both = add(link_sum[lead], mul(staples[lead], view(x_mat, lead, 0, 0)))
        for k in range(2):
            mask = chosen_of[lead]
            for i in range(3):
                for j in range(3):
                    value = jnp.where(mask, straight[k][i, j], grads[lead][k][i, j])
                    value = value + both[0][j, i] if k == 0 else value - both[1][j, i]
                    for x in range(2):
                        link_grad[lead, k, i, j, x] = value[4 * x : 4 * x + 2, :]
                        link_grad[lead + 1, k, i, j, x] = value[4 * x + 2 : 4 * x + 4, :]

    finish(copies_d)
    for dxdt in range(9):
        cut = slice(dxdt * 8, dxdt * 8 + 8)
        for j in range(8):
            kernel_grad[dxdt * 9 + j] = total[j, 0:4, cut]
        for o in range(4):
            kernel_grad[dxdt * 9 + 8, o : o + 1, :] = total[o, 4:5, cut]

    for copy in (
        link_copies + feat_copies + g_copies + k_copies
        + copies_a + copies_b + copies_c + copies_d
    ):
        copy.wait_send()


def shards(sizes, links, kernel, active, direction, out_grad):
    n_space, n_tm, n_low, scale = sizes
    n_high = n_space // n_low
    own_chunks = 8 // n_tm
    red_count = 2 * n_tm + n_low + n_high
    vmem = pl.BlockSpec(memory_space=pltpu.VMEM)

    def space(*shape):
        return pltpu.VMEM(shape, F32)

    def sems(count):
        return pltpu.SemaphoreType.DMA((count,))

    link_grad, kernel_grad = pl.pallas_call(
        functools.partial(body, sizes),
        out_shape=(
            jax.ShapeDtypeStruct(links.shape, F32),
            jax.ShapeDtypeStruct((81, 4, 8), F32),
        ),
        in_specs=[vmem] * 5,
        out_specs=(vmem, vmem),
        scratch_shapes=[
            space(4, 2, 3, 3, GROWS, 128),
            space(4, 2, 2, 3, 2, 128),
            space(3, 2, 2, 3, 2, 128),
            space(2, 2, 2, 3, 1, 128),
            space(4, 2, 2, 3, 2, 128),
            space(3, 2, 2, 3, 2, 128),
            space(4, 2, 2, 3, 2, 128),
            space(3, 2, 2, 3, 2, 128),
            space(2, 2, 2, 3, 1, 128),
            space(12, 2, 3, 3, 8, 128),
            space(9, 36, 8, 128),
            space(4, 4, 8, 128),
            space(9, 16, 8, 128),
            space(64, 128),
            space(3, 8, 128),
            space(64, 128),
            space(4, 4, 8, 128),
            space(3, 3, 8, 128),
            space(9, 2, 3, 3, 8, 128),
            space(GROWS, 128),
            space(8 * GROWS, 128),
            space(4, 2, 3, 3, GROWS, 128),
            space(4, 2, 3, 3, GROWS, 128),
            space(8, 8, 128),
            space(n_tm, own_chunks, 8, 128),
            space(n_low, own_chunks, 8, 128),
            space(n_high, own_chunks, 8, 128),
            space(8, 8, 128),
            sems(6), sems(6), sems(8), sems(8), sems(8), sems(8), sems(6), sems(6),
            sems(red_count), sems(red_count),
        ],
        compiler_params=pltpu.CompilerParams(
            collective_id=0, has_side_effects=True, vmem_limit_bytes=48 * 1024 * 1024
        ),
    )(links, kernel.reshape(81, 4, 8), active, direction, out_grad)
    return (link_grad, kernel_grad.reshape(kernel.shape))


def solution(mesh):
    n_space, n_tm = mesh.shape["space"], mesh.shape["tm"]
    n_low = 1 << ((n_space.bit_length() - 1) // 2)
    sites = n_space * n_tm * 4 * 128
    placed = (
        P(None, None, None, None, "space", "tm", None),
        P(),
        P("space", "tm", None),
        P("space", "tm", None),
        P(None, None, None, None, "space", "tm", None),
    )
    return jax.shard_map(
        functools.partial(shards, (n_space, n_tm, n_low, 1.0 / math.sqrt(sites))),
        mesh=mesh,
        in_specs=placed,
        out_specs=(P(None, None, None, None, "space", "tm", None), P()),
        check_vma=False,
    )
```

profile of v0, /device:TPU:1, one launch (start us, length us, event | category | flops | bytes accessed | tf_op | source)
XLA Modules:
  0.0 65.0 jit_solution(8744991558015130697)
XLA Ops:
  0.6 0.0 copy-start
  0.6 0.9 %copy-done = f32[3,3,3,3,4,8]{5,4,3,2,1,0:T(4,128)S(1)} copy-done((f32[3,3,3,3,4,8]{5,4,3,2,1,0:T(4,128)S(1)}, f32[3,3,3,3,4,8]{5,4,3,2,1,0:T(4,128)}, u32[]{:S(2)}) %copy-start) | copy-done | bytes 10392
  1.5 0.0 copy-start.1
  1.6 0.9 %copy-done.1 = f32[4,2,3,3,2,2,128]{6,5,4,3,2,1,0:T(2,128)S(1)} copy-done((f32[4,2,3,3,2,2,128]{6,5,4,3,2,1,0:T(2,128)S(1)}, f32[4,2,3,3,2,2,128]{6,5,4,3,2,1,0:T(2,128)}, u32[]{:S(2)}) %copy-start.1) | copy-done | bytes 147480
  2.5 0.0 copy-start.2
  2.5 0.9 %copy-done.2 = f32[4,2,3,3,2,2,128]{6,5,4,3,2,1,0:T(2,128)S(1)} copy-done((f32[4,2,3,3,2,2,128]{6,5,4,3,2,1,0:T(2,128)S(1)}, f32[4,2,3,3,2,2,128]{6,5,4,3,2,1,0:T(2,128)}, u32[]{:S(2)}) %copy-start.2) | copy-done | bytes 147480
  3.4 0.0 copy-start.3
  3.4 0.7 %copy-done.3 = s32[2,2,128]{2,1,0:T(2,128)S(1)} copy-done((s32[2,2,128]{2,1,0:T(2,128)S(1)}, s32[2,2,128]{2,1,0:T(2,128)}, u32[]{:S(2)}) %copy-start.3) | copy-done | bytes 2072
  4.1 0.0 copy-start.4
  4.1 0.7 %copy-done.4 = s32[2,2,128]{2,1,0:T(2,128)S(1)} copy-done((s32[2,2,128]{2,1,0:T(2,128)S(1)}, s32[2,2,128]{2,1,0:T(2,128)}, u32[]{:S(2)}) %copy-start.4) | copy-done | bytes 2072
  4.7 59.0 %shard_map.68 = (f32[4,2,3,3,2,2,128]{6,5,4,3,2,1,0:T(2,128)S(1)}, f32[81,4,8]{2,1,0:T(4,128)S(1)}) custom-call(f32[4,2,3,3,2,2,128]{6,5,4,3,2,1,0:T(2,128)S(1)} %copy-done.1, f32[81,4,8]{2,1,0:T(4,128)S(1)} %bitcast.2, s32[2,2,128]{2,1,0:T(2,128)S(1)} %copy-done.3, s32[2,2,128]{2,1,0:T(2,128)S(1)} %copy-done.4, f32[4,2,3,3,2,2,128]{6,5,4,3,2,1,0:T(2,128)S(1)} %copy-done.2), custom_call_target="tpu_custom_call" | custom-call | tf_op jit(solution)/shard_map/pallas_call | solution.py:744
  63.7 0.7 %copy.9 = f32[4,2,3,3,2,2,128]{6,5,4,3,2,1,0:T(2,128)} copy(f32[4,2,3,3,2,2,128]{6,5,4,3,2,1,0:T(2,128)S(1)} %get-tuple-element.8) | data formatting | bytes 294912
  64.4 0.7 %copy.10 = f32[3,3,3,3,4,8]{5,4,3,2,1,0:T(4,128)} copy(f32[3,3,3,3,4,8]{5,4,3,2,1,0:T(4,128)S(1)} %bitcast.3) | data formatting | bytes 20736
Async XLA Ops:
  0.6 0.9 %copy-start = (f32[3,3,3,3,4,8]{5,4,3,2,1,0:T(4,128)S(1)}, f32[3,3,3,3,4,8]{5,4,3,2,1,0:T(4,128)}, u32[]{:S(2)}) copy-start(f32[3,3,3,3,4,8]{5,4,3,2,1,0:T(4,128)} %param.6) | copy-start | bytes 31108
  1.5 0.9 %copy-start.1 = (f32[4,2,3,3,2,2,128]{6,5,4,3,2,1,0:T(2,128)S(1)}, f32[4,2,3,3,2,2,128]{6,5,4,3,2,1,0:T(2,128)}, u32[]{:S(2)}) copy-start(f32[4,2,3,3,2,2,128]{6,5,4,3,2,1,0:T(2,128)} %links.1) | copy-start | bytes 442372
  2.5 0.9 %copy-start.2 = (f32[4,2,3,3,2,2,128]{6,5,4,3,2,1,0:T(2,128)S(1)}, f32[4,2,3,3,2,2,128]{6,5,4,3,2,1,0:T(2,128)}, u32[]{:S(2)}) copy-start(f32[4,2,3,3,2,2,128]{6,5,4,3,2,1,0:T(2,128)} %out_grad.1) | copy-start | bytes 442372
  3.4 0.7 %copy-start.3 = (s32[2,2,128]{2,1,0:T(2,128)S(1)}, s32[2,2,128]{2,1,0:T(2,128)}, u32[]{:S(2)}) copy-start(s32[2,2,128]{2,1,0:T(2,128)} %active.1) | copy-start | bytes 6148
  4.1 0.7 %copy-start.4 = (s32[2,2,128]{2,1,0:T(2,128)S(1)}, s32[2,2,128]{2,1,0:T(2,128)}, u32[]{:S(2)}) copy-start(s32[2,2,128]{2,1,0:T(2,128)} %direction.1) | copy-start | bytes 6148
where the time goes:
time: 65.3 us; the launch traced here: 65 us
  Pallas kernels  59 us (90%)
  local copies, waits for them, and re-layouts  5.42 us (8%)
    pallas_call x1, Pallas kernels, shards(): pl.pallas_call(functools.partial(body, sizes), out_shape=(jax.ShapeDtypeS...  59 us
    unnamed x12, local copies, waits for them, and re-layouts  5.42 us

commit v1 on v0

--- a/solution.py
+++ b/solution.py
@@ -161,39 +161,70 @@
 
 
 def body(
-    sizes, links, taps, active, direction, out_grad, link_grad, kernel_grad,
-    ext, send_t0, send_t1, send_c, recv_x0, recv_x1, recv_t0, recv_t1, recv_c,
+    sizes, links_in, taps_in, active_in, direction_in, out_grad_in, link_grad, kernel_grad,
+    links, taps, active, direction, out_grad,
+    ext, send_x0, send_x1, send_t0, send_t1, send_c, recv_x0, recv_x1, recv_t0, recv_t1, recv_c,
     mids, tap_rows, feats, feat_rows, trace_rows, small, k_rows, k_ext, g_ext, g_rows,
-    code_ext, x_rows, x_mat, dressed, part, red_a, red_b, red_c, total,
-    link_send, link_recv, feat_send, feat_recv, g_send, g_recv, k_send, k_recv,
+    code_ext, x_rows, x_mat, dressed, total, reds,
+    in_sems, link_send, link_recv, feat_send, feat_recv, g_send, g_recv, k_send, k_recv,
     red_send, red_recv,
 ):
-    n_space, n_tm, n_low, scale = sizes
-    n_high = n_space // n_low
+    n_space, n_tm, axes, scale = sizes
+    n_x, n_y, n_far, n_near = axes
+    n_z = n_far * n_near
     my_x, my_t = lax.axis_index("space"), lax.axis_index("tm")
-    low, high = lax.rem(my_x, n_low), lax.div(my_x, n_low)
-    own_chunks = 8 // n_tm
 
     def device(sx, st):
         return (lax.rem(my_x + sx + n_space, n_space), lax.rem(my_t + st + n_tm, n_tm))
 
-    def tm_peer(k):
-        return (my_x, lax.rem(my_t + k, n_tm))
-
-    def low_peer(k):
-        return (high * n_low + lax.rem(low + k, n_low), my_t)
-
-    def high_peer(k):
-        return (lax.rem(high + k, n_high) * n_low + low, my_t)
-
+    at_core = lax.rem(my_t, 2)
+    at_z = lax.rem(my_x, n_far) * n_near + lax.div(my_t, 2)
+    at_y = lax.rem(lax.div(my_x, n_far), n_y)
+    at_x = lax.div(my_x, n_far * n_y)
+
+    def core_peer(k):
+        return (my_x, my_t + 1 - 2 * at_core)
+
+    def z_peer(k):
+        z = lax.rem(at_z + k, n_z)
+        space = lax.div(my_x, n_far) * n_far + lax.div(z, n_near)
+        return (space, lax.rem(z, n_near) * 2 + at_core)
+
+    def y_peer(k):
+        y = lax.rem(at_y + k, n_y)
+        return ((at_x * n_y + y) * n_far + lax.rem(my_x, n_far), my_t)
+
+    def x_peer(k):
+        return (lax.rem(at_x + k, n_x) * n_y * n_far + lax.rem(my_x, n_y * n_far), my_t)
+
+    stages = [
+        (core_peer, at_core, 2, 0),
+        (z_peer, at_z, n_z, 2),
+        (y_peer, at_y, n_y, 2 + n_z),
+        (x_peer, at_x, n_x, 2 + n_z + n_y),
+    ]
     peers = [device(sx, st) for sx, st in NEIGHBOURS]
-    peers += [tm_peer(k) for k in range(2, n_tm - 1)]
-    peers += [low_peer(k) for k in range(1, n_low)]
-    peers += [high_peer(k) for k in range(1, n_high)]
+    for peer_of, _, count, _ in stages:
+        peers += [peer_of(k) for k in range(1, count)]
     barrier = pltpu.get_barrier_semaphore()
     for peer in peers:
         pl.semaphore_signal(barrier, inc=1, device_id=peer, device_id_type=MESH)
 
+    loads = [
+        pltpu.make_async_copy(source, target, in_sems.at[i])
+        for i, (source, target) in enumerate(
+            (
+                (links_in, links), (taps_in, taps), (active_in, active),
+                (direction_in, direction), (out_grad_in, out_grad),
+            )
+        )
+    ]
+    for load in loads:
+        load.start()
+    loads[0].wait()
+
+    send_x0[...] = links[:, :, 0:2, :, 1]
+    send_x1[...] = links[1:4, :, 0:2, :, 0]
     for x in range(2):
         send_t0[:, :, :, :, x : x + 1, :] = links[:, :, 0:2, :, x, 1:2, :]
         send_t1[0:1, :, :, :, x : x + 1, :] = links[0:1, :, 0:2, :, x, 0:1, :]
@@ -219,8 +250,8 @@
             copy.wait_recv()
 
     plan = (
-        (links.at[:, :, 0:2, :, 1], recv_x0, (1, 0)),
-        (links.at[1:4, :, 0:2, :, 0], recv_x1, (-1, 0)),
+        (send_x0, recv_x0, (1, 0)),
+        (send_x1, recv_x1, (-1, 0)),
         (send_c.at[0], recv_c.at[0], (-1, 1)),
         (send_c.at[1], recv_c.at[1], (1, -1)),
         (send_t0, recv_t0, (0, 1)),
@@ -236,6 +267,8 @@
     ext[:, :, :, :, pl.ds(row_of(1, 1), 2), :] = links[:, :, :, :, 0]
     ext[:, :, :, :, pl.ds(row_of(2, 1), 2), :] = links[:, :, :, :, 1]
 
+    for load in loads[1:]:
+        load.wait()
     diagonal = lax.broadcasted_iota(jnp.int32, (8, 8), 0) == lax.broadcasted_iota(
         jnp.int32, (8, 8), 1
     )
@@ -446,21 +479,32 @@
 
     small[0] = course_of.astype(F32)
 
+    def conv_step(own):
+        def step(j, acc):
+            acc = list(acc)
+            for dx in range(3):
+                for dt in range(3):
+                    for o in range(4):
+                        tap = None
+                        for n in range(4):
+                            spot = (n // 2 + dx, n % 2 + dt)
+                            if (spot in inner) != own:
+                                continue
+                            if tap is None:
+                                tap = tap_rows[j, (dx * 3 + dt) * 4 + o]
+                            term = tap * feat_rows[j, spot[0] * 4 + spot[1]]
+                            acc[o * 4 + n] = acc[o * 4 + n] + term
+            return tuple(acc)
+
+        return step
+
+    acc = tuple(jnp.zeros((8, 128), F32) for _ in range(16))
+    acc = lax.fori_loop(0, 9, conv_step(True), acc)
+
     finish(feat_copies)
     roll_features(outer)
 
-    def conv_step(j, acc):
-        acc = list(acc)
-        for dx in range(3):
-            for dt in range(3):
-                for o in range(4):
-                    tap = tap_rows[j, (dx * 3 + dt) * 4 + o]
-                    for n in range(4):
-                        x, t = n // 2, n % 2
-                        acc[o * 4 + n] = acc[o * 4 + n] + tap * feat_rows[j, (x + dx) * 4 + t + dt]
-        return tuple(acc)
-
-    acc = lax.fori_loop(0, 9, conv_step, tuple(jnp.zeros((8, 128), F32) for _ in range(16)))
+    acc = lax.fori_loop(0, 9, conv_step(False), acc)
     for n in range(4):
         s = 4 * (n // 2) + n % 2
         course_row = jnp.broadcast_to(small[0, pl.ds(s, 1), :], (8, 128))
@@ -498,91 +542,100 @@
     )
     k_copies = edge_copies(k_ext, FACES + CORNERS, k_send, k_recv)
 
-    small[2] = field_grad
     sub = lax.broadcasted_iota(jnp.int32, (8, 128), 0).astype(F32)
+    rough = field_grad.astype(jnp.bfloat16).astype(F32)
+    small[2] = rough
+    small[1] = field_grad - rough
     wide = []
     for n in range(4):
         s = 4 * (n // 2) + n % 2
         course_row = jnp.broadcast_to(small[0, pl.ds(s, 1), :], (8, 128))
-        grad_row = jnp.broadcast_to(small[2, pl.ds(s, 1), :], (8, 128))
-        wide.append(jnp.where(course_row == sub, grad_row, 0.0))
-    wide = jnp.concatenate(wide, axis=1)
-
-    def tap_grad(j):
-        lines = []
-        for dx in range(3):
-            for dt in range(3):
+        rough_row = jnp.broadcast_to(small[2, pl.ds(s, 1), :], (8, 128))
+        rest_row = jnp.broadcast_to(small[1, pl.ds(s, 1), :], (8, 128))
+        wide.append(
+            jnp.where(course_row == sub, rough_row, 0.0)
+            + jnp.where(course_row + 4.0 == sub, rest_row, 0.0)
+        )
+    wide = jnp.concatenate(wide, axis=1).astype(jnp.bfloat16)
+    lines = []
+    for dx in range(3):
+        for dt in range(3):
+            for j in range(9):
                 lines.append(
                     jnp.concatenate(
-                        [
-                            feat_rows[j, (n // 2 + dx) * 4 + n % 2 + dt]
-                            for n in range(4)
-                        ],
-                        axis=1,
+                        [feat_rows[j, (n // 2 + dx) * 4 + n % 2 + dt] for n in range(4)], axis=1
                     )
                 )
-        return lax.dot_general(
-            wide, jnp.concatenate(lines, axis=0), (((1,), (1,)), ((), ())),
-            precision=lax.Precision.HIGHEST, preferred_element_type=F32,
-        )
-
-    part[...] = jnp.zeros((8, 8, 128), F32)
-
-    def tap_step(j, carry):
-        part[j, :, 0:72] = tap_grad(j)
-        return carry
-
-    lax.fori_loop(0, 8, tap_step, 0)
-    last = tap_grad(8)
-    for o in range(4):
-        part[o, 4:5, 0:72] = last[o : o + 1, :]
-
-    red_a[my_t] = part[pl.ds(my_t * own_chunks, own_chunks)]
-    base_a, base_b, base_c, base_d = 0, n_tm, n_tm + n_low, n_tm + n_low + n_high
-    copies_a = []
-    for k in range(1, n_tm):
-        peer = tm_peer(k)
-        copies_a.append(
-            remote(
-                part.at[pl.ds(peer[1] * own_chunks, own_chunks)], red_a.at[my_t],
-                red_send.at[base_a + k], red_recv.at[base_a + k], peer,
-            )
-        )
-    start_all(copies_a)
-
-    decay = powers[4]
+    lines = jnp.concatenate(lines + [jnp.zeros((8, 512), F32)], axis=0)
+    lines_high = lines.astype(jnp.bfloat16)
+    lines_low = (lines - lines_high.astype(F32)).astype(jnp.bfloat16)
+    contract = (((1,), (1,)), ((), ()))
+    high_sum = lax.dot_general(wide, lines_high, contract, preferred_element_type=F32)
+    low_sum = lax.dot_general(wide, lines_low, contract, preferred_element_type=F32)
+    tap_sum = high_sum[0:4] + (high_sum[4:8] + low_sum[0:4])
+    total[...] = jnp.zeros((4, 768), F32)
+    total[:, 0:656] = tap_sum
+
+    def send_stage(number, value):
+        peer_of, place, count, base = stages[number]
+        buffer = reds[number]
+        buffer[place] = value
+        return start_all(
+            [
+                remote(
+                    buffer.at[place], buffer.at[place],
+                    red_send.at[base + k], red_recv.at[base + k], peer_of(k),
+                )
+                for k in range(1, count)
+            ]
+        )
+
+    def take_stage(number, copies):
+        finish(copies)
+        buffer = reds[number]
+        out = buffer[0]
+        for k in range(1, stages[number][2]):
+            out = out + buffer[k]
+        return out
+
+    copies_a = send_stage(0, total[...])
+
     blend = scaled(powers[4], 1.0 / 24.0)
     for k, factor in ((3, 1.0 / 6.0), (2, 0.5), (1, 1.0), (0, 1.0)):
         blend = add(scaled(blend, strength), scaled(powers[k], factor))
     straight = mul(blend, picked_link)
 
-    finish(g_copies)
-
-    whole = g_ext[...]
-    axis = whole.ndim - 2
-    mask = half_mask(whole.shape)
-    values = jnp.where(mask, pltpu.roll(whole, 2, axis), whole)
-    codes = jnp.where(mask, whole, pltpu.roll(whole, 6, axis))
-    for pair in range(2):
-        wanted = jnp.where(mask, 2.0 * pair + 1.0, 2.0 * pair)
-        one = jnp.where(codes == wanted, values, 0.0)
-        for dy in range(3):
-            along_y = shift_yz(one, 1 - dy, 0)
-            for dz in range(3):
-                g_rows[dy * 3 + dz, pair] = shift_yz(along_y, 0, 1 - dz)
+    def spread_blocks(blocks, places):
+        mask = half_mask(blocks.shape)
+        axis = blocks.ndim - 2
+        values = jnp.where(mask, pltpu.roll(blocks, 2, axis), blocks)
+        codes = jnp.where(mask, blocks, pltpu.roll(blocks, 6, axis))
+        for pair in range(2):
+            wanted = jnp.where(mask, 2.0 * pair + 1.0, 2.0 * pair)
+            one = jnp.where(codes == wanted, values, 0.0)
+            for dy in range(3):
+                along_y = shift_yz(one, 1 - dy, 0)
+                for dz in range(3):
+                    moved = shift_yz(along_y, 0, 1 - dz)
+                    for n, (bx, bt) in enumerate(places):
+                        g_rows[dy * 3 + dz, pair, bx, bt] = moved[n]
 
     spots = inner + [(0, 1), (0, 2), (3, 1), (3, 2), (1, 0), (2, 0), (1, 3), (2, 3), (3, 0), (0, 3)]
 
-    def back_step(spot_list):
+    def back_step(own):
         def step(j, acc):
             acc = list(acc)
             for o in range(4):
                 rows = {}
                 for dx in range(3):
                     for dt in range(3):
-                        tap = tap_rows[j, (dx * 3 + dt) * 4 + o]
-                        for n, (ext_x, ext_t) in enumerate(spot_list):
+                        tap = None
+                        for n, (ext_x, ext_t) in enumerate(spots):
                             px, pt = ext_x + 2 - dx, ext_t + 2 - dt
+                            if (px // 2 == 1 and pt // 2 == 1) != own:
+                                continue
+                            if tap is None:
+                                tap = tap_rows[j, (dx * 3 + dt) * 4 + o]
                             if (px, pt) not in rows:
                                 s = 4 * (px % 2) + 2 * (o % 2) + pt % 2
                                 rows[px, pt] = jnp.broadcast_to(
@@ -593,9 +646,16 @@
 
         return step
 
-    spot_grad = lax.fori_loop(
-        0, 9, back_step(spots), tuple(jnp.zeros((8, 128), F32) for _ in spots)
-    )
+    around = [(bx, bt) for bx in range(3) for bt in range(3) if (bx, bt) != (1, 1)]
+    spread_blocks(g_ext[1, 1:2], [(1, 1)])
+    spot_grad = tuple(jnp.zeros((8, 128), F32) for _ in spots)
+    spot_grad = lax.fori_loop(0, 9, back_step(True), spot_grad)
+
+    copies_b = send_stage(1, take_stage(0, copies_a))
+
+    finish(g_copies)
+    spread_blocks(jnp.stack([g_ext[bx, bt] for bx, bt in around]), around)
+    spot_grad = lax.fori_loop(0, 9, back_step(False), spot_grad)
 
     finish(k_copies)
     for n, (ext_x, ext_t) in enumerate(spots):
@@ -635,24 +695,6 @@
                 x_mat[course, k, :, :, rows, :] = matrix[k]
                 dressed[course, k, :, :, rows, :] = product[k]
 
-    def reduce_step(copies, buffer):
-        finish(copies)
-        out = buffer[0]
-        for k in range(1, buffer.shape[0]):
-            out = out + buffer[k]
-        return out
-
-    red_b[low] = reduce_step(copies_a, red_a)
-    copies_b = start_all(
-        [
-            remote(
-                red_b.at[low], red_b.at[low],
-                red_send.at[base_b + k], red_recv.at[base_b + k], low_peer(k),
-            )
-            for k in range(1, n_low)
-        ]
-    )
-
     link_sum = {0: None, 2: None}
 
     def backward(number):
@@ -672,34 +714,13 @@
         both = add(above, below)
         link_sum[course] = both if link_sum[course] is None else add(link_sum[course], both)
 
-    for number in range(3):
+    for number in range(4):
         backward(number)
 
-    red_c[high] = reduce_step(copies_b, red_b)
-    copies_c = start_all(
-        [
-            remote(
-                red_c.at[high], red_c.at[high],
-                red_send.at[base_c + k], red_recv.at[base_c + k], high_peer(k),
-            )
-            for k in range(1, n_high)
-        ]
-    )
-
-    for number in range(3, 6):
+    copies_c = send_stage(2, take_stage(1, copies_b))
+
+    for number in range(4, 6):
         backward(number)
-
-    mine = pl.ds(my_t * own_chunks, own_chunks)
-    total[mine] = reduce_step(copies_c, red_c) * scale
-    copies_d = start_all(
-        [
-            remote(
-                total.at[mine], total.at[mine],
-                red_send.at[base_d + k], red_recv.at[base_d + k], tm_peer(k),
-            )
-            for k in range(1, n_tm)
-        ]
-    )
 
     for lead in (0, 2):
         both = add(link_sum[lead], mul(staples[lead], view(x_mat, lead, 0, 0)))
@@ -713,13 +734,10 @@
                         link_grad[lead, k, i, j, x] = value[4 * x : 4 * x + 2, :]
                         link_grad[lead + 1, k, i, j, x] = value[4 * x + 2 : 4 * x + 4, :]
 
-    finish(copies_d)
-    for dxdt in range(9):
-        cut = slice(dxdt * 8, dxdt * 8 + 8)
-        for j in range(8):
-            kernel_grad[dxdt * 9 + j] = total[j, 0:4, cut]
-        for o in range(4):
-            kernel_grad[dxdt * 9 + 8, o : o + 1, :] = total[o, 4:5, cut]
+    copies_d = send_stage(3, take_stage(2, copies_c))
+    total[...] = take_stage(3, copies_d) * scale
+    for d in range(81):
+        kernel_grad[d] = total[:, d * 8 : d * 8 + 8]
 
     for copy in (
         link_copies + feat_copies + g_copies + k_copies
@@ -729,10 +747,8 @@
 
 
 def shards(sizes, links, kernel, active, direction, out_grad):
-    n_space, n_tm, n_low, scale = sizes
-    n_high = n_space // n_low
-    own_chunks = 8 // n_tm
-    red_count = 2 * n_tm + n_low + n_high
+    n_x, n_y, n_far, n_near = sizes[2]
+    counts = (2, n_far * n_near, n_y, n_x)
     vmem = pl.BlockSpec(memory_space=pltpu.VMEM)
 
     def space(*shape):
@@ -747,10 +763,17 @@
             jax.ShapeDtypeStruct(links.shape, F32),
             jax.ShapeDtypeStruct((81, 4, 8), F32),
         ),
-        in_specs=[vmem] * 5,
+        in_specs=[pl.BlockSpec(memory_space=pltpu.HBM)] * 5,
         out_specs=(vmem, vmem),
         scratch_shapes=[
+            space(4, 2, 3, 3, 2, 2, 128),
+            space(81, 4, 8),
+            pltpu.VMEM((2, 2, 128), jnp.int32),
+            pltpu.VMEM((2, 2, 128), jnp.int32),
+            space(4, 2, 3, 3, 2, 2, 128),
             space(4, 2, 3, 3, GROWS, 128),
+            space(4, 2, 2, 3, 2, 128),
+            space(3, 2, 2, 3, 2, 128),
             space(4, 2, 2, 3, 2, 128),
             space(3, 2, 2, 3, 2, 128),
             space(2, 2, 2, 3, 1, 128),
@@ -773,16 +796,14 @@
             space(8 * GROWS, 128),
             space(4, 2, 3, 3, GROWS, 128),
             space(4, 2, 3, 3, GROWS, 128),
-            space(8, 8, 128),
-            space(n_tm, own_chunks, 8, 128),
-            space(n_low, own_chunks, 8, 128),
-            space(n_high, own_chunks, 8, 128),
-            space(8, 8, 128),
+            space(4, 768),
+            [space(count, 4, 768) for count in counts],
+            sems(5),
             sems(6), sems(6), sems(8), sems(8), sems(8), sems(8), sems(6), sems(6),
-            sems(red_count), sems(red_count),
+            sems(sum(counts)), sems(sum(counts)),
         ],
         compiler_params=pltpu.CompilerParams(
-            collective_id=0, has_side_effects=True, vmem_limit_bytes=48 * 1024 * 1024
+            collective_id=0, has_side_effects=True, vmem_limit_bytes=60 * 1024 * 1024
         ),
     )(links, kernel.reshape(81, 4, 8), active, direction, out_grad)
     return (link_grad, kernel_grad.reshape(kernel.shape))
@@ -790,7 +811,9 @@
 
 def solution(mesh):
     n_space, n_tm = mesh.shape["space"], mesh.shape["tm"]
-    n_low = 1 << ((n_space.bit_length() - 1) // 2)
+    n_far = 2
+    n_x = max(1, n_space // (8 * n_far))
+    axes = (n_x, n_space // (n_x * n_far), n_far, n_tm // 2)
     sites = n_space * n_tm * 4 * 128
     placed = (
         P(None, None, None, None, "space", "tm", None),
@@ -800,7 +823,7 @@
         P(None, None, None, None, "space", "tm", None),
     )
     return jax.shard_map(
-        functools.partial(shards, (n_space, n_tm, n_low, 1.0 / math.sqrt(sites))),
+        functools.partial(shards, (n_space, n_tm, axes, 1.0 / math.sqrt(sites))),
         mesh=mesh,
         in_specs=placed,
         out_specs=(P(None, None, None, None, "space", "tm", None), P()),

time: 65.3 us -> 53 us (0.81)
  Pallas kernels: 59 us -> 49.9 us
  local copies, waits for them, and re-layouts: 5.42 us -> 2.29 us
    pallas_call x1, Pallas kernels: 59 us -> 49.9 us  [shards(): pl.pallas_call(functools.partial(body, sizes), out_shape=(jax.ShapeDtypeS...]
    unnamed x12 -> x4, local copies, waits for them, and re-layouts: 5.42 us -> 2.29 us
where the time goes in v1:
time: 53 us; the launch traced here: 52.9 us
  Pallas kernels  49.9 us (94%)
  local copies, waits for them, and re-layouts  2.29 us (4%)
  between operations  0.65 us (1%)
    pallas_call x1, Pallas kernels, shards(): pl.pallas_call(functools.partial(body, sizes), out_shape=(jax.ShapeDtypeS...  49.9 us
    unnamed x4, local copies, waits for them, and re-layouts  2.29 us

profile of v1, /device:TPU:1, one launch (start us, length us, event | category | flops | bytes accessed | tf_op | source)
XLA Modules:
  0.0 52.9 jit_solution(15921702591762903065)
XLA Ops:
  0.6 49.9 %shard_map.68 = (f32[4,2,3,3,2,2,128]{6,5,4,3,2,1,0:T(2,128)}, f32[81,4,8]{2,1,0:T(4,128)}) custom-call(f32[4,2,3,3,2,2,128]{6,5,4,3,2,1,0:T(2,128)} %links_in.1, f32[81,4,8]{2,1,0:T(4,128)} %bitcast.2, s32[2,2,128]{2,1,0:T(2,128)} %active_in.1, s32[2,2,128]{2,1,0:T(2,128)} %direction_in.1, f32[4,2,3,3,2,2,128]{6,5,4,3,2,1,0:T(2,128)} %out_grad_in.1), custom_call_target="tpu_custom_call" | custom-call | tf_op jit(solution)/shard_map/pallas_call | solution.py:760
  50.6 0.0 copy-start
  50.6 1.6 %copy.9 = f32[4,2,3,3,2,2,128]{6,5,4,3,2,1,0:T(2,128)} copy(f32[4,2,3,3,2,2,128]{6,5,4,3,2,1,0:T(2,128)} %get-tuple-element.8) | data formatting | bytes 294912
  52.2 0.0 copy-done
  52.2 0.7 %copy.10 = f32[3,3,3,3,4,8]{5,4,3,2,1,0:T(4,128)} copy(f32[3,3,3,3,4,8]{5,4,3,2,1,0:T(4,128)S(1)} %bitcast.3) | data formatting | bytes 20736
Async XLA Ops:
  50.6 1.6 %copy-start = (f32[81,4,8]{2,1,0:T(4,128)S(1)}, f32[81,4,8]{2,1,0:T(4,128)}, u32[]{:S(2)}) copy-start(f32[81,4,8]{2,1,0:T(4,128)} %get-tuple-element.5) | copy-start | bytes 31108

commit v2 on v1

--- a/solution.py
+++ b/solution.py
@@ -162,7 +162,7 @@
 
 def body(
     sizes, links_in, taps_in, active_in, direction_in, out_grad_in, link_grad, kernel_grad,
-    links, taps, active, direction, out_grad,
+    links, taps, active, direction, out_grad, grad_out, tap_out,
     ext, send_x0, send_x1, send_t0, send_t1, send_c, recv_x0, recv_x1, recv_t0, recv_t1, recv_c,
     mids, tap_rows, feats, feat_rows, trace_rows, small, k_rows, k_ext, g_ext, g_rows,
     code_ext, x_rows, x_mat, dressed, total, reds,
@@ -182,9 +182,6 @@
     at_y = lax.rem(lax.div(my_x, n_far), n_y)
     at_x = lax.div(my_x, n_far * n_y)
 
-    def core_peer(k):
-        return (my_x, my_t + 1 - 2 * at_core)
-
     def z_peer(k):
         z = lax.rem(at_z + k, n_z)
         space = lax.div(my_x, n_far) * n_far + lax.div(z, n_near)
@@ -195,16 +192,21 @@
         return ((at_x * n_y + y) * n_far + lax.rem(my_x, n_far), my_t)
 
     def x_peer(k):
-        return (lax.rem(at_x + k, n_x) * n_y * n_far + lax.rem(my_x, n_y * n_far), my_t)
-
-    stages = [
-        (core_peer, at_core, 2, 0),
-        (z_peer, at_z, n_z, 2),
-        (y_peer, at_y, n_y, 2 + n_z),
-        (x_peer, at_x, n_x, 2 + n_z + n_y),
-    ]
+        place = lax.rem(at_x * 2 + at_core + k, 2 * n_x)
+        space = lax.div(place, 2) * n_y * n_far + lax.rem(my_x, n_y * n_far)
+        return (space, my_t - at_core + lax.rem(place, 2))
+
+    along_z = (z_peer, at_z, n_z)
+    along_y = (y_peer, at_y, n_y)
+    along_x = (x_peer, at_x * 2 + at_core, 2 * n_x)
+    stages = []
+    base = 0
+    for half in ((along_z, along_y, along_x), (along_y, along_z, along_x)):
+        for peer_of, place, count in half:
+            stages.append((peer_of, place, count, base))
+            base += count
     peers = [device(sx, st) for sx, st in NEIGHBOURS]
-    for peer_of, _, count, _ in stages:
+    for peer_of, _, count in (along_z, along_y, along_x):
         peers += [peer_of(k) for k in range(1, count)]
     barrier = pltpu.get_barrier_semaphore()
     for peer in peers:
@@ -598,7 +600,7 @@
             out = out + buffer[k]
         return out
 
-    copies_a = send_stage(0, total[...])
+    copies_a = [send_stage(3 * h, total[:, 384 * h : 384 * h + 384]) for h in range(2)]
 
     blend = scaled(powers[4], 1.0 / 24.0)
     for k, factor in ((3, 1.0 / 6.0), (2, 0.5), (1, 1.0), (0, 1.0)):
@@ -651,10 +653,9 @@
     spot_grad = tuple(jnp.zeros((8, 128), F32) for _ in spots)
     spot_grad = lax.fori_loop(0, 9, back_step(True), spot_grad)
 
-    copies_b = send_stage(1, take_stage(0, copies_a))
-
     finish(g_copies)
     spread_blocks(jnp.stack([g_ext[bx, bt] for bx, bt in around]), around)
+    copies_b = [send_stage(3 * h + 1, take_stage(3 * h, copies_a[h])) for h in range(2)]
     spot_grad = lax.fori_loop(0, 9, back_step(False), spot_grad)
 
     finish(k_copies)
@@ -714,12 +715,7 @@
         both = add(above, below)
         link_sum[course] = both if link_sum[course] is None else add(link_sum[course], both)
 
-    for number in range(4):
-        backward(number)
-
-    copies_c = send_stage(2, take_stage(1, copies_b))
-
-    for number in range(4, 6):
+    for number in range(6):
         backward(number)
 
     for lead in (0, 2):
@@ -731,25 +727,33 @@
                     value = jnp.where(mask, straight[k][i, j], grads[lead][k][i, j])
                     value = value + both[0][j, i] if k == 0 else value - both[1][j, i]
                     for x in range(2):
-                        link_grad[lead, k, i, j, x] = value[4 * x : 4 * x + 2, :]
-                        link_grad[lead + 1, k, i, j, x] = value[4 * x + 2 : 4 * x + 4, :]
-
-    copies_d = send_stage(3, take_stage(2, copies_c))
-    total[...] = take_stage(3, copies_d) * scale
+                        grad_out[lead, k, i, j, x] = value[4 * x : 4 * x + 2, :]
+                        grad_out[lead + 1, k, i, j, x] = value[4 * x + 2 : 4 * x + 4, :]
+
+    store_links = pltpu.make_async_copy(grad_out, link_grad, in_sems.at[0])
+    store_links.start()
+    copies_c = [send_stage(3 * h + 2, take_stage(3 * h + 1, copies_b[h])) for h in range(2)]
+    for h in range(2):
+        total[:, 384 * h : 384 * h + 384] = take_stage(3 * h + 2, copies_c[h]) * scale
     for d in range(81):
-        kernel_grad[d] = total[:, d * 8 : d * 8 + 8]
+        tap_out[d] = total[:, d * 8 : d * 8 + 8]
+    store_taps = pltpu.make_async_copy(tap_out, kernel_grad, in_sems.at[1])
+    store_taps.start()
+    store_links.wait()
+    store_taps.wait()
 
     for copy in (
         link_copies + feat_copies + g_copies + k_copies
-        + copies_a + copies_b + copies_c + copies_d
+        + sum(copies_a + copies_b + copies_c, [])
     ):
         copy.wait_send()
 
 
 def shards(sizes, links, kernel, active, direction, out_grad):
     n_x, n_y, n_far, n_near = sizes[2]
-    counts = (2, n_far * n_near, n_y, n_x)
-    vmem = pl.BlockSpec(memory_space=pltpu.VMEM)
+    n_z = n_far * n_near
+    counts = (n_z, n_y, 2 * n_x, n_y, n_z, 2 * n_x)
+    hbm = pl.BlockSpec(memory_space=pltpu.HBM)
 
     def space(*shape):
         return pltpu.VMEM(shape, F32)
@@ -763,14 +767,16 @@
             jax.ShapeDtypeStruct(links.shape, F32),
             jax.ShapeDtypeStruct((81, 4, 8), F32),
         ),
-        in_specs=[pl.BlockSpec(memory_space=pltpu.HBM)] * 5,
-        out_specs=(vmem, vmem),
+        in_specs=[hbm] * 5,
+        out_specs=(hbm, hbm),
         scratch_shapes=[
             space(4, 2, 3, 3, 2, 2, 128),
             space(81, 4, 8),
             pltpu.VMEM((2, 2, 128), jnp.int32),
             pltpu.VMEM((2, 2, 128), jnp.int32),
             space(4, 2, 3, 3, 2, 2, 128),
+            space(4, 2, 3, 3, 2, 2, 128),
+            space(81, 4, 8),
             space(4, 2, 3, 3, GROWS, 128),
             space(4, 2, 2, 3, 2, 128),
             space(3, 2, 2, 3, 2, 128),
@@ -797,7 +803,7 @@
             space(4, 2, 3, 3, GROWS, 128),
             space(4, 2, 3, 3, GROWS, 128),
             space(4, 768),
-            [space(count, 4, 768) for count in counts],
+            [space(count, 4, 384) for count in counts],
             sems(5),
             sems(6), sems(6), sems(8), sems(8), sems(8), sems(8), sems(6), sems(6),
             sems(sum(counts)), sems(sum(counts)),

time: 53 us -> 52.1 us (0.983)
  Pallas kernels: 49.9 us -> 49 us
    pallas_call x1, Pallas kernels: 49.9 us -> 49 us  [shards(): pl.pallas_call(functools.partial(body, sizes), out_shape=(jax.ShapeDtypeS...]
where the time goes in v2:
time: 52.1 us; the launch traced here: 52 us
  Pallas kernels  49 us (94%)
  local copies, waits for them, and re-layouts  2.29 us (4%)
  between operations  0.65 us (1%)
    pallas_call x1, Pallas kernels, shards(): pl.pallas_call(functools.partial(body, sizes), out_shape=(jax.ShapeDtypeS...  49 us
    unnamed x4, local copies, waits for them, and re-layouts  2.29 us

profile of v2, /device:TPU:1, one launch (start us, length us, event | category | flops | bytes accessed | tf_op | source)
XLA Modules:
  0.0 52.0 jit_solution(2178527580061081488)
XLA Ops:
  0.6 49.0 %shard_map.68 = (f32[4,2,3,3,2,2,128]{6,5,4,3,2,1,0:T(2,128)}, f32[81,4,8]{2,1,0:T(4,128)}) custom-call(f32[4,2,3,3,2,2,128]{6,5,4,3,2,1,0:T(2,128)} %links_in.1, f32[81,4,8]{2,1,0:T(4,128)} %bitcast.2, s32[2,2,128]{2,1,0:T(2,128)} %active_in.1, s32[2,2,128]{2,1,0:T(2,128)} %direction_in.1, f32[4,2,3,3,2,2,128]{6,5,4,3,2,1,0:T(2,128)} %out_grad_in.1), custom_call_target="tpu_custom_call" | custom-call | tf_op jit(solution)/shard_map/pallas_call | solution.py:764
  49.7 0.0 copy-start
  49.7 1.6 %copy.9 = f32[4,2,3,3,2,2,128]{6,5,4,3,2,1,0:T(2,128)} copy(f32[4,2,3,3,2,2,128]{6,5,4,3,2,1,0:T(2,128)} %get-tuple-element.8) | data formatting | bytes 294912
  51.3 0.0 copy-done
  51.3 0.7 %copy.10 = f32[3,3,3,3,4,8]{5,4,3,2,1,0:T(4,128)} copy(f32[3,3,3,3,4,8]{5,4,3,2,1,0:T(4,128)S(1)} %bitcast.3) | data formatting | bytes 20736
Async XLA Ops:
  49.7 1.6 %copy-start = (f32[81,4,8]{2,1,0:T(4,128)S(1)}, f32[81,4,8]{2,1,0:T(4,128)}, u32[]{:S(2)}) copy-start(f32[81,4,8]{2,1,0:T(4,128)} %get-tuple-element.5) | copy-start | bytes 31108

commit v3 on v2

--- a/solution.py
+++ b/solution.py
@@ -201,7 +201,7 @@
     along_x = (x_peer, at_x * 2 + at_core, 2 * n_x)
     stages = []
     base = 0
-    for half in ((along_z, along_y, along_x), (along_y, along_z, along_x)):
+    for half in ((along_x, along_z, along_y), (along_x, along_y, along_z)):
         for peer_of, place, count in half:
             stages.append((peer_of, place, count, base))
             base += count
@@ -506,7 +506,7 @@
     finish(feat_copies)
     roll_features(outer)
 
-    acc = lax.fori_loop(0, 9, conv_step(False), acc)
+    acc = lax.fori_loop(0, 9, conv_step(False), acc, unroll=9)
     for n in range(4):
         s = 4 * (n // 2) + n % 2
         course_row = jnp.broadcast_to(small[0, pl.ds(s, 1), :], (8, 128))
@@ -653,10 +653,11 @@
     spot_grad = tuple(jnp.zeros((8, 128), F32) for _ in spots)
     spot_grad = lax.fori_loop(0, 9, back_step(True), spot_grad)
 
+    copies_b = [send_stage(3 * h + 1, take_stage(3 * h, copies_a[h])) for h in range(2)]
+
     finish(g_copies)
     spread_blocks(jnp.stack([g_ext[bx, bt] for bx, bt in around]), around)
-    copies_b = [send_stage(3 * h + 1, take_stage(3 * h, copies_a[h])) for h in range(2)]
-    spot_grad = lax.fori_loop(0, 9, back_step(False), spot_grad)
+    spot_grad = lax.fori_loop(0, 9, back_step(False), spot_grad, unroll=3)
 
     finish(k_copies)
     for n, (ext_x, ext_t) in enumerate(spots):
@@ -736,7 +737,7 @@
     for h in range(2):
         total[:, 384 * h : 384 * h + 384] = take_stage(3 * h + 2, copies_c[h]) * scale
     for d in range(81):
-        tap_out[d] = total[:, d * 8 : d * 8 + 8]
+        tap_out[d // 27, d // 9 % 3, d // 3 % 3, d % 3] = total[:, d * 8 : d * 8 + 8]
     store_taps = pltpu.make_async_copy(tap_out, kernel_grad, in_sems.at[1])
     store_taps.start()
     store_links.wait()
@@ -752,7 +753,7 @@
 def shards(sizes, links, kernel, active, direction, out_grad):
     n_x, n_y, n_far, n_near = sizes[2]
     n_z = n_far * n_near
-    counts = (n_z, n_y, 2 * n_x, n_y, n_z, 2 * n_x)
+    counts = (2 * n_x, n_z, n_y, 2 * n_x, n_y, n_z)
     hbm = pl.BlockSpec(memory_space=pltpu.HBM)
 
     def space(*shape):
@@ -765,7 +766,7 @@
         functools.partial(body, sizes),
         out_shape=(
             jax.ShapeDtypeStruct(links.shape, F32),
-            jax.ShapeDtypeStruct((81, 4, 8), F32),
+            jax.ShapeDtypeStruct(kernel.shape, F32),
         ),
         in_specs=[hbm] * 5,
         out_specs=(hbm, hbm),
@@ -776,7 +777,7 @@
             pltpu.VMEM((2, 2, 128), jnp.int32),
             space(4, 2, 3, 3, 2, 2, 128),
             space(4, 2, 3, 3, 2, 2, 128),
-            space(81, 4, 8),
+            space(*kernel.shape),
             space(4, 2, 3, 3, GROWS, 128),
             space(4, 2, 2, 3, 2, 128),
             space(3, 2, 2, 3, 2, 128),
@@ -812,7 +813,7 @@
             collective_id=0, has_side_effects=True, vmem_limit_bytes=60 * 1024 * 1024
         ),
     )(links, kernel.reshape(81, 4, 8), active, direction, out_grad)
-    return (link_grad, kernel_grad.reshape(kernel.shape))
+    return (link_grad, kernel_grad)
 
 
 def solution(mesh):

time: 52.1 us -> 50 us (0.960)
  Pallas kernels: 49 us -> 46.9 us
    pallas_call x1, Pallas kernels: 49 us -> 46.9 us  [shards(): pl.pallas_call(functools.partial(body, sizes), out_shape=(jax.ShapeDtypeS...]
where the time goes in v3:
time: 50 us; the launch traced here: 49.9 us
  Pallas kernels  46.9 us (94%)
  local copies, waits for them, and re-layouts  2.29 us (5%)
  between operations  0.65 us (1%)
    pallas_call x1, Pallas kernels, shards(): pl.pallas_call(functools.partial(body, sizes), out_shape=(jax.ShapeDtypeS...  46.9 us
    unnamed x4, local copies, waits for them, and re-layouts  2.29 us

profile of v3, /device:TPU:1, one launch (start us, length us, event | category | flops | bytes accessed | tf_op | source)
XLA Modules:
  0.0 49.9 jit_solution(15126001164587357563)
XLA Ops:
  0.6 46.9 %shard_map.68 = (f32[4,2,3,3,2,2,128]{6,5,4,3,2,1,0:T(2,128)}, f32[3,3,3,3,4,8]{5,4,3,2,1,0:T(4,128)}) custom-call(f32[4,2,3,3,2,2,128]{6,5,4,3,2,1,0:T(2,128)} %links_in.1, f32[81,4,8]{2,1,0:T(4,128)} %bitcast.1, s32[2,2,128]{2,1,0:T(2,128)} %active_in.1, s32[2,2,128]{2,1,0:T(2,128)} %direction_in.1, f32[4,2,3,3,2,2,128]{6,5,4,3,2,1,0:T(2,128)} %out_grad_in.1), custom_call_target="tpu_custom_call" | custom-call | tf_op jit(solution)/shard_map/pallas_call | solution.py:765
  47.6 0.0 copy-start
  47.6 1.6 %copy.9 = f32[4,2,3,3,2,2,128]{6,5,4,3,2,1,0:T(2,128)} copy(f32[4,2,3,3,2,2,128]{6,5,4,3,2,1,0:T(2,128)} %get-tuple-element.4) | data formatting | bytes 294912
  49.2 0.0 copy-done
  49.2 0.7 %copy.10 = f32[3,3,3,3,4,8]{5,4,3,2,1,0:T(4,128)} copy(f32[3,3,3,3,4,8]{5,4,3,2,1,0:T(4,128)S(1)} %copy-done) | data formatting | bytes 20736
Async XLA Ops:
  47.6 1.6 %copy-start = (f32[3,3,3,3,4,8]{5,4,3,2,1,0:T(4,128)S(1)}, f32[3,3,3,3,4,8]{5,4,3,2,1,0:T(4,128)}, u32[]{:S(2)}) copy-start(f32[3,3,3,3,4,8]{5,4,3,2,1,0:T(4,128)} %get-tuple-element.5) | copy-start | bytes 31108

commit v4 on v3

--- a/solution.py
+++ b/solution.py
@@ -748,6 +748,24 @@
         + sum(copies_a + copies_b + copies_c, [])
     ):
         copy.wait_send()
+
+
+def hand_on(link_in, kernel_in, link_out, kernel_out, link_held, kernel_held, sems):
+    loads = [
+        pltpu.make_async_copy(link_in, link_held, sems.at[0]),
+        pltpu.make_async_copy(kernel_in, kernel_held, sems.at[1]),
+    ]
+    stores = [
+        pltpu.make_async_copy(link_held, link_out, sems.at[2]),
+        pltpu.make_async_copy(kernel_held, kernel_out, sems.at[3]),
+    ]
+    for load in loads:
+        load.start()
+    for load, store in zip(loads, stores):
+        load.wait()
+        store.start()
+    for store in stores:
+        store.wait()
 
 
 def shards(sizes, links, kernel, active, direction, out_grad):
@@ -813,7 +831,17 @@
             collective_id=0, has_side_effects=True, vmem_limit_bytes=60 * 1024 * 1024
         ),
     )(links, kernel.reshape(81, 4, 8), active, direction, out_grad)
-    return (link_grad, kernel_grad)
+    return pl.pallas_call(
+        hand_on,
+        out_shape=(
+            jax.ShapeDtypeStruct(links.shape, F32),
+            jax.ShapeDtypeStruct(kernel.shape, F32),
+        ),
+        in_specs=[hbm] * 2,
+        out_specs=(hbm, hbm),
+        scratch_shapes=[space(*links.shape), space(*kernel.shape), sems(4)],
+        compiler_params=pltpu.CompilerParams(vmem_limit_bytes=60 * 1024 * 1024),
+    )(link_grad, kernel_grad)
 
 
 def solution(mesh):

time: 50 us -> 49.4 us (0.988)
  local copies, waits for them, and re-layouts: 2.29 us -> 0 us
  Pallas kernels: 46.9 us -> 48.6 us
    unnamed x4 -> x0, local copies, waits for them, and re-layouts: 2.29 us -> none
    pallas_call x0 -> x1, Pallas kernels: none -> 1.69 us  [shards(): pl.pallas_call(hand_on, out_shape=(jax.ShapeDtypeStruct(links.shape, F32)...]
where the time goes in v4:
time: 49.4 us; the launch traced here: 49.3 us
  Pallas kernels  48.6 us (98%)
  between operations  0.64 us (1%)
    pallas_call x1, Pallas kernels, shards(): pl.pallas_call(functools.partial(body, sizes), out_shape=(jax.ShapeDtypeS...  46.9 us
    pallas_call x1, Pallas kernels, shards(): pl.pallas_call(hand_on, out_shape=(jax.ShapeDtypeStruct(links.shape, F32)...  1.69 us

profile of v4, /device:TPU:1, one launch (start us, length us, event | category | flops | bytes accessed | tf_op | source)
XLA Modules:
  0.0 49.3 jit_solution(11338275829161844900)
XLA Ops:
  0.6 46.9 %shard_map.68 = (f32[4,2,3,3,2,2,128]{6,5,4,3,2,1,0:T(2,128)}, f32[3,3,3,3,4,8]{5,4,3,2,1,0:T(4,128)}) custom-call(f32[4,2,3,3,2,2,128]{6,5,4,3,2,1,0:T(2,128)} %links_in.1, f32[81,4,8]{2,1,0:T(4,128)} %bitcast.1, s32[2,2,128]{2,1,0:T(2,128)} %active_in.1, s32[2,2,128]{2,1,0:T(2,128)} %direction_in.1, f32[4,2,3,3,2,2,128]{6,5,4,3,2,1,0:T(2,128)} %out_grad_in.1), custom_call_target="tpu_custom_call" | custom-call | tf_op jit(solution)/shard_map/pallas_call | solution.py:783
  47.6 1.7 %shard_map.69 = (f32[4,2,3,3,2,2,128]{6,5,4,3,2,1,0:T(2,128)}, f32[3,3,3,3,4,8]{5,4,3,2,1,0:T(4,128)}) custom-call(f32[4,2,3,3,2,2,128]{6,5,4,3,2,1,0:T(2,128)} %get-tuple-element.4.link_in, f32[3,3,3,3,4,8]{5,4,3,2,1,0:T(4,128)} %get-tuple-element.5.kernel_in), custom_call_target="tpu_custom_call" | custom-call | tf_op jit(solution)/shard_map/pallas_call | solution.py:834

commit v5 on v4

--- a/solution.py
+++ b/solution.py
@@ -522,28 +522,6 @@
     slope = c1 + strength * (c2 + strength * (c3 * 0.5 + strength * (c4 * (1.0 / 6.0))))
     field_grad = moves * (1.0 - bent * bent) * slope
     code = jnp.where(moving == 1, course_of, -1).astype(F32)
-    g_ext[1, 1] = jnp.where(hid == 0, field_grad, code)
-    t1, t2, t3, t4 = turns
-    for k in range(8):
-        poly = t1[k] + strength * (
-            t2[k] * 0.5 + strength * (t3[k] * (1.0 / 6.0) + strength * (t4[k] * (1.0 / 24.0)))
-        )
-        k_rows[pl.ds(8 * k, 8), :] = -strength * poly
-    for x in range(2):
-        for t in range(2):
-            k_ext[1 + x, 1 + t] = k_rows[pl.ds(4 * x + t, 8, 8), :]
-
-    g_copies = start_all(
-        [
-            remote(
-                g_ext.at[1, 1], g_ext.at[1 - sx, 1 - st],
-                g_send.at[i], g_recv.at[i], device(sx, st),
-            )
-            for i, (sx, st) in enumerate(NEIGHBOURS)
-        ]
-    )
-    k_copies = edge_copies(k_ext, FACES + CORNERS, k_send, k_recv)
-
     sub = lax.broadcasted_iota(jnp.int32, (8, 128), 0).astype(F32)
     rough = field_grad.astype(jnp.bfloat16).astype(F32)
     small[2] = rough
@@ -601,6 +579,28 @@
         return out
 
     copies_a = [send_stage(3 * h, total[:, 384 * h : 384 * h + 384]) for h in range(2)]
+
+    g_ext[1, 1] = jnp.where(hid == 0, field_grad, code)
+    t1, t2, t3, t4 = turns
+    for k in range(8):
+        poly = t1[k] + strength * (
+            t2[k] * 0.5 + strength * (t3[k] * (1.0 / 6.0) + strength * (t4[k] * (1.0 / 24.0)))
+        )
+        k_rows[pl.ds(8 * k, 8), :] = -strength * poly
+    for x in range(2):
+        for t in range(2):
+            k_ext[1 + x, 1 + t] = k_rows[pl.ds(4 * x + t, 8, 8), :]
+
+    g_copies = start_all(
+        [
+            remote(
+                g_ext.at[1, 1], g_ext.at[1 - sx, 1 - st],
+                g_send.at[i], g_recv.at[i], device(sx, st),
+            )
+            for i, (sx, st) in enumerate(NEIGHBOURS)
+        ]
+    )
+    k_copies = edge_copies(k_ext, FACES + CORNERS, k_send, k_recv)
 
     blend = scaled(powers[4], 1.0 / 24.0)
     for k, factor in ((3, 1.0 / 6.0), (2, 0.5), (1, 1.0), (0, 1.0)):
@@ -716,8 +716,12 @@
         both = add(above, below)
         link_sum[course] = both if link_sum[course] is None else add(link_sum[course], both)
 
-    for number in range(6):
+    for number in range(5):
         backward(number)
+
+    copies_c = [send_stage(3 * h + 2, take_stage(3 * h + 1, copies_b[h])) for h in range(2)]
+
+    backward(5)
 
     for lead in (0, 2):
         both = add(link_sum[lead], mul(staples[lead], view(x_mat, lead, 0, 0)))
@@ -733,7 +737,6 @@
 
     store_links = pltpu.make_async_copy(grad_out, link_grad, in_sems.at[0])
     store_links.start()
-    copies_c = [send_stage(3 * h + 2, take_stage(3 * h + 1, copies_b[h])) for h in range(2)]
     for h in range(2):
         total[:, 384 * h : 384 * h + 384] = take_stage(3 * h + 2, copies_c[h]) * scale
     for d in range(81):

time: 49.4 us -> 49.5 us (level)
  no operation moved by 1% of the time
where the time goes in v5:
time: 49.5 us; the launch traced here: 49.4 us
  Pallas kernels  48.7 us (98%)
  between operations  0.64 us (1%)
    pallas_call x1, Pallas kernels, shards(): pl.pallas_call(functools.partial(body, sizes), out_shape=(jax.ShapeDtypeS...  47 us
    pallas_call x1, Pallas kernels, shards(): pl.pallas_call(hand_on, out_shape=(jax.ShapeDtypeStruct(links.shape, F32)...  1.69 us

profile of v5, /device:TPU:1, one launch (start us, length us, event | category | flops | bytes accessed | tf_op | source)
XLA Modules:
  0.0 49.4 jit_solution(9793843243499117679)
XLA Ops:
  0.6 47.0 %shard_map.68 = (f32[4,2,3,3,2,2,128]{6,5,4,3,2,1,0:T(2,128)}, f32[3,3,3,3,4,8]{5,4,3,2,1,0:T(4,128)}) custom-call(f32[4,2,3,3,2,2,128]{6,5,4,3,2,1,0:T(2,128)} %links_in.1, f32[81,4,8]{2,1,0:T(4,128)} %bitcast.1, s32[2,2,128]{2,1,0:T(2,128)} %active_in.1, s32[2,2,128]{2,1,0:T(2,128)} %direction_in.1, f32[4,2,3,3,2,2,128]{6,5,4,3,2,1,0:T(2,128)} %out_grad_in.1), custom_call_target="tpu_custom_call" | custom-call | tf_op jit(solution)/shard_map/pallas_call | solution.py:786
  47.7 1.7 %shard_map.69 = (f32[4,2,3,3,2,2,128]{6,5,4,3,2,1,0:T(2,128)}, f32[3,3,3,3,4,8]{5,4,3,2,1,0:T(4,128)}) custom-call(f32[4,2,3,3,2,2,128]{6,5,4,3,2,1,0:T(2,128)} %get-tuple-element.4.link_in, f32[3,3,3,3,4,8]{5,4,3,2,1,0:T(4,128)} %get-tuple-element.5.kernel_in), custom_call_target="tpu_custom_call" | custom-call | tf_op jit(solution)/shard_map/pallas_call | solution.py:837
